TPU v7x, 256 devices: a whole 4x4x8 slice. The times are simulated.
256 devices in a mesh: dp: 64 (over z, y, core), mp: 4 (over x).
Axes of the slice: x: 4, y: 4, z: 8, core: 2. Of those that a mesh axis runs over, the one named last changes fastest.
Arguments:
- grads: bfloat16 [4, 32, 1024, 1024], P('mp', None, 'dp')
- momentum: float32 [4, 32, 1024, 1024], P('mp', None, 'dp'), may hold values from -6 to 6
- root_factors: float32 [4, 64, 1024, 1024], P('mp', 'dp'), as said below
- owner_table: int32 [4, 32], P('mp'), may hold values from 0 to 31, each once within a row
Outputs:
- new_momentum: float32 [4, 32, 1024, 1024], P('mp', None, 'dp')
- direction: bfloat16 [4, 32, 1024, 1024], P('mp', None, 'dp')
Inputs may be any that keep to these rules, and one draw needn't show every extreme that they name: `owner_table`: each row names each of the 32 factor pairs once. `root_factors`: each slot holds a symmetric positive definite matrix.
All inputs are finite; a program needn't handle non-finite values.
Results may differ from a plain program's by a relative error of at most 0.0006.
Values may be sent and summed in bfloat16 or wider, within the bound.
A program may use at most 64 MiB of HBM per device.

v0:
```python
import jax
import jax.numpy as jnp
from jax import lax
from jax.sharding import PartitionSpec as P


def from_partner(block, axis, stride):
    count = lax.axis_size(axis)
    route = []
    for low in range(count):
        high = low | 1 << stride
        if high != low and high < count:
            route += [(low, high), (high, low)]
    return lax.ppermute(block, axis, route)


def matmul_f32(first_matrix, second_matrix):
    return jnp.dot(first_matrix, second_matrix, precision=lax.Precision.HIGHEST)


def per_device(grads, momentum, root_factors, owner_table):
    dp_count = lax.axis_size("dp")
    my_index = lax.axis_index("dp")
    is_even = my_index % 2 == 0
    my_pair = my_index // 2
    pair_table = owner_table[0]
    blocks = pair_table.shape[0]
    row_count = grads.shape[2]
    block_order = grads.shape[3]
    local_rows = grads[0]
    positions = jnp.arange(blocks, dtype=jnp.int32)
    matches = pair_table[None, :] == positions[:, None]
    block_of_pair = jnp.sum(jnp.where(matches, positions[None, :], 0), axis=1)
    targets = block_of_pair[jnp.arange(dp_count, dtype=jnp.int32) // 2]
    outgoing = jnp.take(local_rows, targets, axis=0)
    incoming = lax.all_to_all(outgoing, "dp", split_axis=0, concat_axis=0, tiled=True)
    full_block = incoming.reshape(dp_count * row_count, block_order).astype(jnp.float32)
    own_factor = root_factors[0, 0]
    first_product = lax.cond(
        is_even,
        lambda: matmul_f32(own_factor, full_block),
        lambda: matmul_f32(full_block, own_factor),
    )
    partner = from_partner(first_product, "dp", 0)
    left_factor = jnp.where(is_even, own_factor, partner)
    right_factor = jnp.where(is_even, partner, own_factor)
    regrouped = left_factor.reshape(dp_count, 2, row_count // 2, block_order)
    own_half = lax.dynamic_index_in_dim(regrouped, my_index % 2, 1, keepdims=False)
    precond = matmul_f32(own_half.reshape(dp_count * (row_count // 2), block_order), right_factor)
    grad_sq = jnp.sum(jnp.square(local_rows.astype(jnp.float32)), axis=(1, 2))
    own_sq = jnp.sum(jnp.square(precond))
    pre_sq = jnp.where(pair_table == my_pair, own_sq, jnp.float32(0.0))
    grad_total, pre_total = lax.psum((grad_sq, pre_sq), ("dp", "mp"))
    graft_ratio = jnp.sqrt(grad_total) / (jnp.sqrt(pre_total) + 1e-06)
    outgoing_back = precond.reshape(dp_count, row_count // 2, block_order)
    returned = lax.all_to_all(outgoing_back, "dp", split_axis=0, concat_axis=0, tiled=True)
    by_pair = returned.reshape(blocks, row_count, block_order)
    update = jnp.take(by_pair, pair_table, axis=0) * graft_ratio[:, None, None]
    new_momentum = 0.9 * momentum[0] + update
    direction = (update + 0.9 * new_momentum).astype(jnp.bfloat16)
    return (new_momentum[None], direction[None])


def solution(mesh):
    in_specs = (
        P("mp", None, "dp", None),
        P("mp", None, "dp", None),
        P("mp", "dp", None, None),
        P("mp", None),
    )
    out_specs = (P("mp", None, "dp", None), P("mp", None, "dp", None))
    return jax.shard_map(
        per_device, mesh=mesh, in_specs=in_specs, out_specs=out_specs, check_vma=False
    )
```

profile of v0, /device:TPU:1, one launch (start us, length us, event | category | flops | bytes accessed | tf_op | source)
XLA Modules:
  0.0 213.6 jit_solution(15344103778652199297)
XLA Ops:
  0.7 0.8 select_reduce_fusion
  1.4 0.8 gather_fusion
  2.2 1.9 gather_fusion.1
  4.2 1.6 broadcast_select_fusion
  5.7 13.2 %all-to-all-start = ((bf16[64,16,1024]{2,1,0:T(8,128)(2,1)}), bf16[64,16,1024]{2,1,0:T(8,128)(2,1)S(1)}, u32[]{:S(2)}, u32[]{:S(2)}) async-start(bf16[64,16,1024]{2,1,0:T(8,128)(2,1)} %broadcast_select_fusion), calls=%async_computation | async-start | bytes 4194304 | tf_op jit(solution)/shard_map/all_to_all | solution.py:36
  18.9 49.7 %all-to-all-done = bf16[64,16,1024]{2,1,0:T(8,128)(2,1)S(1)} async-done(((bf16[64,16,1024]{2,1,0:T(8,128)(2,1)}), bf16[64,16,1024]{2,1,0:T(8,128)(2,1)S(1)}, u32[]{:S(2)}, u32[]{:S(2)}) %all-to-all-start) | async-done | bytes 2097184 | tf_op jit(solution)/shard_map/all_to_all | solution.py:36
  68.6 0.0 copy-start
  68.6 0.6 bitcast_convert_fusion
  69.2 1.6 copy-done
  70.8 14.7 %conditional.1 = (f32[1024,1024]{1,0:T(8,128)}) conditional(s32[]{:T(128)} %convert_element_type.16, (f32[1024,1024]{1,0:T(8,128)S(1)}, f32[1024,1024]{1,0:T(8,128)S(1)}) %tuple.21, (f32[1024,1024]{1,0:T(8,128)S(1)}, f32[1024,1024]{1,0:T(8,128)S(1)}) %tuple.22), branch_computations={%region_1.2_spmd, %region_2.3_spmd} | conditional | flops 12884901888 | bytes 12582920 | solution.py:39
  70.8 14.7 %fusion.11 = f32[1024,1024]{1,0:T(8,128)} fusion(f32[1024,1024]{1,0:T(8,128)S(1)} %get-tuple-element.8, f32[1024,1024]{1,0:T(8,128)S(1)} %get-tuple-element.12), kind=kOutput, calls=%fused_computation.40 | convolution fusion | flops 12884901888 | bytes 12582912 | tf_op jit(solution)/shard_map/cond/branch_0_fun/dot_general | solution.py:18
  85.5 2.1 %collective-permute-start = (f32[1024,1024]{1,0:T(8,128)}, f32[1024,1024]{1,0:T(8,128)}, u32[]{:S(2)}, u32[]{:S(2)}) collective-permute-start(f32[1024,1024]{1,0:T(8,128)} %get-tuple-element.23), channel_id=1, source_target_pairs={{0,4},{4,0},{8,12},{12,8},{16,20},{20,16},{24,28},{28,24},{32,36},... | collective-permute-start | bytes 12582920 | tf_op jit(solution)/shard_map/ppermute | solution.py:14
  87.6 7.1 %collective-permute-done = f32[1024,1024]{1,0:T(8,128)} collective-permute-done((f32[1024,1024]{1,0:T(8,128)}, f32[1024,1024]{1,0:T(8,128)}, u32[]{:S(2)}, u32[]{:S(2)}) %collective-permute-start) | collective-permute-done | bytes 4194336 | tf_op jit(solution)/shard_map/ppermute | solution.py:14
  94.8 0.0 copy-start.1
  94.8 4.6 %broadcast_select_fusion.1 = f32[1024,1024]{1,0:T(8,128)S(1)} fusion(f32[1024,1024]{1,0:T(8,128)} %collective-permute-done, pred[]{:T(512)S(6)} %eq.25, f32[1,1,1024,1024]{3,2,1,0:T(8,128)} %param.8), kind=kLoop, calls=%fused_computation.16 | loop fusion | flops 1048576 | bytes 12582913 | tf_op jit(solution)/shard_map/jit(_where)/select_n | solution.py:45
  99.3 0.1 copy-done.1
  99.4 9.1 %multiply_reduce_fusion = (f32[]{:T(128)}, f32[512,1024]{1,0:T(8,128)}) fusion(f32[1024,1024]{1,0:T(8,128)} %collective-permute-done, pred[]{:T(512)S(6)} %eq.25, f32[1,1,1024,1024]{3,2,1,0:T(8,128)S(1)} %copy-done.1, f32[64,2,8,1024]{3,2,1,0:T(8,128)S(1)} %bitcast.49, s32[]{:T(128)S(6)} %select_n.116), kind=kOutput, calls=%fused_computation.10 | convolution fusion | flops 6444548096 | bytes 12582921 | tf_op jit(solution)/shard_map/dot_general | solution.py:18
  108.4 0.0 copy-start.2
  108.4 0.0 copy-start.3
  108.4 5.8 %all-to-all-start.1 = ((f32[64,8,1024]{2,1,0:T(8,128)}), f32[64,8,1024]{2,1,0:T(8,128)S(1)}, u32[]{:S(2)}, u32[]{:S(2)}) async-start(f32[64,8,1024]{2,1,0:T(8,128)} %bitcast.10), calls=%async_computation.1 | async-start | bytes 4194304 | tf_op jit(solution)/shard_map/all_to_all | solution.py:56
  114.3 0.0 copy-done.2
  114.3 0.4 multiply_reduce_fusion.1
  114.6 0.0 copy-done.3
  114.7 0.7 compare_select_fusion.5
  115.3 91.7 %all-reduce = (f32[32]{0:T(128)S(1)}, f32[32]{0:T(128)S(1)}) all-reduce(f32[32]{0:T(128)S(1)} %compare_select_fusion.5, f32[32]{0:T(128)S(1)} %multiply_reduce_fusion.1), channel_id=1, replica_groups=mesh['dp'=64,'mp'=4] {'dp','mp'}, use_global_device_ids=true, to_apply=%region_6.7 | all-reduce | flops 64 | bytes 512 | tf_op jit(solution)/shard_map/psum | solution.py:53
  207.0 0.0 all-to-all-done.1
  207.0 2.0 gather_fusion.2
  209.0 4.6 %add_convert_fusion = (bf16[1,32,16,1024]{3,2,1,0:T(8,128)(2,1)}, f32[1,32,16,1024]{3,2,1,0:T(8,128)}) fusion(f32[32,16,1024]{2,1,0:T(8,128)} %gather_fusion.2, f32[32]{0:T(128)S(1)} %add_divide_fusion, pred[32]{0:T(512)(128)(4,1)S(1)} %compare_and_fusion.1, f32[1,32,16,1024]{3,2,1,0:T(8,128)} %param.7), kind=kLoop, calls=%fused_computation.9 | loop fusion | flops 3670016 | bytes 7340192 | tf_op jit(solution)/shard_map/convert_element_type | solution.py:60
  (9 shorter events, 0.1 us)
Async XLA Ops:
  5.7 62.8 %all-to-all-start = ((bf16[64,16,1024]{2,1,0:T(8,128)(2,1)}), bf16[64,16,1024]{2,1,0:T(8,128)(2,1)S(1)}, u32[]{:S(2)}, u32[]{:S(2)}) async-start(bf16[64,16,1024]{2,1,0:T(8,128)(2,1)} %broadcast_select_fusion), calls=%async_computation | async-start | bytes 4194304 | tf_op jit(solution)/shard_map/all_to_all | solution.py:36
  68.6 2.2 %copy-start = (f32[1,1,1024,1024]{3,2,1,0:T(8,128)S(1)}, f32[1,1,1024,1024]{3,2,1,0:T(8,128)}, u32[]{:S(2)}) copy-start(f32[1,1,1024,1024]{3,2,1,0:T(8,128)} %param.8) | copy-start | bytes 12582916
  85.5 9.3 %collective-permute-start = (f32[1024,1024]{1,0:T(8,128)}, f32[1024,1024]{1,0:T(8,128)}, u32[]{:S(2)}, u32[]{:S(2)}) collective-permute-start(f32[1024,1024]{1,0:T(8,128)} %get-tuple-element.23), channel_id=1, source_target_pairs={{0,4},{4,0},{8,12},{12,8},{16,20},{20,16},{24,28},{28,24},{32,36},... | collective-permute-start | bytes 12582920 | tf_op jit(solution)/shard_map/ppermute | solution.py:14
  94.8 4.6 %copy-start.1 = (f32[1,1,1024,1024]{3,2,1,0:T(8,128)S(1)}, f32[1,1,1024,1024]{3,2,1,0:T(8,128)}, u32[]{:S(2)}) copy-start(f32[1,1,1024,1024]{3,2,1,0:T(8,128)} %param.8) | copy-start | bytes 12582916
  108.4 5.8 %copy-start.2 = (bf16[1,32,16,1024]{3,2,1,0:T(8,128)(2,1)S(1)}, bf16[1,32,16,1024]{3,2,1,0:T(8,128)(2,1)}, u32[]{:S(2)}) copy-start(bf16[1,32,16,1024]{3,2,1,0:T(8,128)(2,1)} %param.6) | copy-start | bytes 3145732
  108.4 6.2 %copy-start.3 = (s32[1,32]{1,0:T(1,128)S(1)}, s32[1,32]{1,0:T(1,128)}, u32[]{:S(2)}) copy-start(s32[1,32]{1,0:T(1,128)} %param.9) | copy-start | bytes 388
  108.4 98.6 %all-to-all-start.1 = ((f32[64,8,1024]{2,1,0:T(8,128)}), f32[64,8,1024]{2,1,0:T(8,128)S(1)}, u32[]{:S(2)}, u32[]{:S(2)}) async-start(f32[64,8,1024]{2,1,0:T(8,128)} %bitcast.10), calls=%async_computation.1 | async-start | bytes 4194304 | tf_op jit(solution)/shard_map/all_to_all | solution.py:56
where the time goes:
time: 214 us
  blocking collectives  91.7 us (43%)
  waiting for transfers between devices  56.8 us (27%)
  matrix products  23.8 us (11%)
  starting transfers between devices  21.1 us (10%)
  other arithmetic  13.2 us (6%)
  local copies, waits for them, and re-layouts  6.37 us (3%)
    psum x1, blocking collectives, per_device(): grad_total, pre_total = lax.psum((grad_sq, pre_sq), ('dp', 'mp'))  91.7 us
    all_to_all x1, waiting for transfers between devices, per_device(): lax.all_to_all(outgoing, 'dp', split_axis=0, concat_axis=0, tiled=True)  49.7 us
    dot_general x2, matrix products, matmul_f32(): return jnp.dot(first_matrix, second_matrix, precision=lax.Precision.HIGHEST)  23.8 us
    all_to_all x1, starting transfers between devices, per_device(): lax.all_to_all(outgoing, 'dp', split_axis=0, concat_axis=0, tiled=True)  13.2 us
    ppermute x1, waiting for transfers between devices, from_partner(): return lax.ppermute(block, axis, route)  7.13 us
    all_to_all x1, starting transfers between devices, per_device(): lax.all_to_all(outgoing_back, 'dp', split_axis=0, concat_axis=0, tiled=True)  5.79 us
    convert_element_type x1, other arithmetic, per_device(): direction = (update + 0.9 * new_momentum).astype(jnp.bfloat16)  4.61 us
    select_n x1, other arithmetic, per_device(): left_factor = jnp.where(is_even, own_factor, partner)  4.55 us
  transfers between devices with their start and end apart: 3, of which 2 were waited for; matrix products, arithmetic and copies ran while one was open for 0% of the time, Pallas kernels for 0%

commit v1 on v0

v1 whole, which is shorter than its diff:
```python
import jax
import jax.numpy as jnp
from jax import lax
from jax.experimental import pallas as pl
from jax.experimental.pallas import tpu as pltpu
from jax.sharding import PartitionSpec as P

Z, Y, X = 8, 4, 4
PAIRS = Z * Y
ROWS = 16
B = 1024
HALF = B // 2
LANES = 128
TOP = 32767.0
MESH = pl.DeviceIdType.MESH
F32 = jnp.float32
BF16 = jnp.bfloat16
OFFSETS = (0, 1, 7, 2, 6, 3, 5, 4)


def offset_at(i):
    step = (i + 1) // 2
    return lax.rem(step + (1 - i % 2) * (8 - 2 * step), 8)


def block_of(owner_ref, pair):
    found = jnp.int32(0)
    for b in range(PAIRS):
        found = jnp.where(owner_ref[0, b] == pair, b, found)
    return found


def exchange_kernel(
    owner_ref, grads_ref, factor_hbm,
    back_ref, head_ref,
    factor, outgoing, gathered, left, right, left_other, product, coded, heads, sums, seen,
    factor_sem, grad_send, grad_recv, sib_send, sib_recv, fac_send, fac_recv,
    back_send, back_recv, sum_send, sum_recv, head_send, head_recv, local_sem, head_local,
):
    me = lax.axis_index("dp")
    x = lax.axis_index("mp")
    z = me // (2 * Y)
    y = (me // 2) % Y
    c = me % 2
    pair = me // 2
    sibling = {"dp": pair * 2 + (1 - c)}

    def chip(i, dy):
        return lax.rem(z + Z - offset_at(i), Z) * Y + lax.rem(y + dy, Y)

    barrier = pltpu.get_barrier_semaphore()

    @pl.loop(1, PAIRS)
    def _(s):
        k = chip(s // Y, s % Y)
        pl.semaphore_signal(barrier, inc=1, device_id={"dp": k * 2 + c}, device_id_type=MESH)

    pl.semaphore_signal(barrier, inc=1, device_id=sibling, device_id_type=MESH)

    @pl.loop(2, 2 * X)
    def _(s):
        target = {"dp": pair * 2 + lax.rem(c + s, 2), "mp": lax.rem(x + s // 2, X)}
        pl.semaphore_signal(barrier, inc=1, device_id=target, device_id_type=MESH)

    factor_in = pltpu.make_async_copy(factor_hbm, factor, factor_sem)
    factor_in.start()

    @pl.loop(0, PAIRS)
    def _(s):
        outgoing[s] = grads_ref[block_of(owner_ref, chip(s // Y, s % Y))]

    pl.semaphore_wait(barrier, (PAIRS - 1) + 1 + (2 * X - 2))

    own_rows = pltpu.make_async_copy(outgoing.at[0], gathered.at[0, y, c], local_sem)
    own_rows.start()

    @pl.loop(1, PAIRS)
    def _(s):
        i = s // Y
        pltpu.make_async_remote_copy(
            src_ref=outgoing.at[s], dst_ref=gathered.at[i, y, c],
            send_sem=grad_send, recv_sem=grad_recv.at[i],
            device_id={"dp": chip(i, s % Y) * 2 + c}, device_id_type=MESH,
        ).start()

    factor_in.wait()

    def split(part_ref, at, value):
        high = value.astype(BF16)
        part_ref[(0,) + at] = high
        part_ref[(1,) + at] = (value - high.astype(F32)).astype(BF16)

    @pl.when(c == 0)
    def _():
        @pl.loop(0, Z)
        def _(i):
            zi = lax.rem(z + offset_at(i), Z)
            for j in range(Z):
                zj = lax.rem(z + OFFSETS[j], Z)
                cols = pl.ds(pl.multiple_of(zj * LANES, LANES), LANES)
                to = pl.ds(j * LANES, LANES)
                split(left, (i, slice(None), slice(None), to), factor[zi, :, 0, :, cols])
                split(left_other, (i, slice(None), slice(None), to), factor[zi, :, 1, :, cols])
            pltpu.make_async_remote_copy(
                src_ref=left_other.at[:, i], dst_ref=left.at[:, i],
                send_sem=fac_send, recv_sem=fac_recv,
                device_id=sibling, device_id_type=MESH,
            ).start()

    @pl.when(c == 1)
    def _():
        @pl.loop(0, Z)
        def _(i):
            for q in range(Y):
                for h in range(2):
                    split(right, (i, q, h), factor[i, q, h])
            pltpu.make_async_remote_copy(
                src_ref=right.at[:, i], dst_ref=right.at[:, i],
                send_sem=fac_send, recv_sem=fac_recv,
                device_id=sibling, device_id_type=MESH,
            ).start()

    def whole(ref, send, recv):
        return pltpu.make_async_remote_copy(
            src_ref=ref, dst_ref=ref, send_sem=send, recv_sem=recv,
            device_id=sibling, device_id_type=MESH,
        )

    own_rows.wait()

    def pass_on(i):
        @pl.when(i == 0)
        def _():
            whole(gathered.at[0, pl.ds(0, Y - 1), 0], grad_send, grad_recv.at[0]).wait_recv()

        @pl.when(i > 0)
        def _():
            whole(gathered.at[i, :, 0], grad_send, grad_recv.at[i]).wait_recv()

        pltpu.make_async_remote_copy(
            src_ref=gathered.at[i, :, c], dst_ref=gathered.at[i, :, c],
            send_sem=sib_send, recv_sem=sib_recv.at[i],
            device_id=sibling, device_id_type=MESH,
        ).start()

    @pl.loop(0, 2)
    def _(i):
        pass_on(i)

    @pl.when(c == 0)
    def _():
        whole(right, fac_send, fac_recv).wait_recv()

    @pl.when(c == 1)
    def _():
        whole(left, fac_send, fac_recv).wait_recv()

    @pl.loop(0, Y)
    def _(j):
        @pl.when(j > 0)
        def _():
            pass_on(2 * j)
            pass_on(2 * j + 1)

        whole(gathered.at[2 * j, :, 0], sib_send, sib_recv.at[2 * j]).wait_recv()
        whole(gathered.at[2 * j + 1, :, 0], sib_send, sib_recv.at[2 * j + 1]).wait_recv()
        some = gathered[pl.ds(2 * j, 2)].reshape(2 * LANES, B)
        cols = pl.ds(pl.multiple_of(j * 2 * LANES, 2 * LANES), 2 * LANES)
        rows = left[:, :, :, :, cols].reshape(B, 2 * LANES)
        term = jnp.dot(rows, some, preferred_element_type=F32)
        term = term[:HALF] + term[HALF:]

        @pl.when(j == 0)
        def _():
            product[...] = term

        @pl.when(j > 0)
        def _():
            product[...] += term

    seen[...] = jnp.zeros_like(seen)
    lane = lax.broadcasted_iota(jnp.int32, (ROWS, LANES), 1)
    diagonal = lane == lax.broadcasted_iota(jnp.int32, (ROWS, LANES), 0)

    @pl.loop(0, Y)
    def _(j):
        base = pl.multiple_of(j * LANES, LANES)
        rows = product[pl.ds(base, LANES)]
        high = rows.astype(BF16)
        low = (rows - high.astype(F32)).astype(BF16)
        both = jnp.concatenate([high, low], axis=0)
        by_high = jnp.dot(both, right[0].reshape(B, B), preferred_element_type=F32)
        by_low = jnp.dot(high, right[1].reshape(B, B), preferred_element_type=F32)
        product[pl.ds(base, LANES)] = by_high[:LANES] + (by_high[LANES:] + by_low)

        @pl.loop(0, 2 * Y)
        def _(q):
            s = j * 2 * Y + q
            value = product[pl.ds(pl.multiple_of(s * ROWS, ROWS), ROWS)]
            seen[...] += _fold(value * value)
            size = jnp.abs(value)
            top = jnp.maximum(jnp.max(size, axis=1, keepdims=True), 1e-37)
            heads[s, 0:1] = jnp.sum(jnp.where(diagonal, jnp.broadcast_to(top, (ROWS, LANES)), 0.0), axis=0, keepdims=True)
            code = (jnp.sqrt(size * (1.0 / top)) * TOP + 0.5).astype(jnp.int32)
            code = jnp.where(value < 0.0, -code, code)
            coded[s] = (code[:, :HALF] & 0xFFFF) | (code[:, HALF:] << 16)
            i = s // Y
            k = lax.rem(z + offset_at(i), Z) * Y + s % Y

            @pl.when(k != pair)
            def _():
                pltpu.make_async_remote_copy(
                    src_ref=coded.at[s], dst_ref=back_ref.at[pair],
                    send_sem=back_send, recv_sem=back_recv,
                    device_id={"dp": k * 2 + c}, device_id_type=MESH,
                ).start()

            @pl.when(k == pair)
            def _():
                pltpu.make_async_copy(coded.at[s], back_ref.at[pair], local_sem).start()

    block = block_of(owner_ref, pair)

    def grad_sum(i, total):
        rows = gathered[i, :, pl.ds(c, 1)].reshape(Y * ROWS, B).astype(F32)
        return total + _fold(rows * rows)

    grad_sq = jnp.sum(lax.fori_loop(0, Z, grad_sum, jnp.zeros((8, LANES), F32)))
    pre_sq = jnp.sum(seen[...])
    one = lax.broadcasted_iota(jnp.int32, (1, LANES), 1)
    sums[0] = jnp.where(one == block, pre_sq, 0.0) + jnp.where(one == block + 64, grad_sq, 0.0)

    @pl.loop(1, 2 * X)
    def _(s):
        target = {"dp": pair * 2 + lax.rem(c + s, 2), "mp": lax.rem(x + s // 2, X)}
        pltpu.make_async_remote_copy(
            src_ref=sums.at[0], dst_ref=sums.at[s],
            send_sem=sum_send, recv_sem=sum_recv,
            device_id=target, device_id_type=MESH,
        ).start()

    whole(sums.at[pl.ds(1, 2 * X - 1)], sum_send, sum_recv).wait()
    total = jnp.sum(sums[...], axis=0)

    @pl.loop(0, PAIRS)
    def _(s):
        heads[s, 1:2] = total
        k = lax.rem(z + offset_at(s // Y), Z) * Y + s % Y

        @pl.when(k != pair)
        def _():
            pltpu.make_async_remote_copy(
                src_ref=heads.at[s], dst_ref=head_ref.at[pair],
                send_sem=head_send, recv_sem=head_recv,
                device_id={"dp": k * 2 + c}, device_id_type=MESH,
            ).start()

        @pl.when(k == pair)
        def _():
            pltpu.make_async_copy(heads.at[s], head_ref.at[pair], head_local).start()

    others = pl.ds(0, PAIRS - 1)
    whole(outgoing.at[others], grad_send, grad_recv.at[0]).wait_send()
    whole(gathered.at[:, :, 0], sib_send, sib_recv.at[0]).wait_send()

    @pl.when(c == 0)
    def _():
        whole(left_other, fac_send, fac_recv).wait_send()

    @pl.when(c == 1)
    def _():
        whole(right, fac_send, fac_recv).wait_send()

    pltpu.make_async_copy(coded.at[0], back_ref.at[pair], local_sem).wait()
    pltpu.make_async_copy(heads.at[0], head_ref.at[pair], head_local).wait()
    whole(back_ref.at[others], back_send, back_recv).wait()
    whole(head_ref.at[others], head_send, head_recv).wait()


def _fold(value):
    total = jnp.zeros((8, LANES), F32)
    for r in range(0, value.shape[0], 8):
        for q in range(0, value.shape[1], LANES):
            total = total + value[r:r + 8, q:q + LANES]
    return total


def exchange(owner, grads, factor):
    grads_words = (PAIRS, ROWS, B)
    return pl.pallas_call(
        exchange_kernel,
        out_shape=(
            jax.ShapeDtypeStruct((PAIRS, ROWS, HALF), jnp.int32),
            jax.ShapeDtypeStruct((PAIRS, 2, LANES), F32),
        ),
        in_specs=[
            pl.BlockSpec(memory_space=pltpu.SMEM),
            pl.BlockSpec(memory_space=pltpu.VMEM),
            pl.BlockSpec(memory_space=pl.ANY),
        ],
        out_specs=[pl.BlockSpec(memory_space=pltpu.VMEM)] * 2,
        scratch_shapes=[
            pltpu.VMEM((Z, Y, 2, ROWS, B), F32),
            pltpu.VMEM(grads_words, BF16),
            pltpu.VMEM((Z, Y, 2, ROWS, B), BF16),
            pltpu.VMEM((2, Z, Y, ROWS, B), BF16),
            pltpu.VMEM((2, Z, Y, 2, ROWS, B), BF16),
            pltpu.VMEM((2, Z, Y, ROWS, B), BF16),
            pltpu.VMEM((HALF, B), F32),
            pltpu.VMEM((PAIRS, ROWS, HALF), jnp.int32),
            pltpu.VMEM((PAIRS, 2, LANES), F32),
            pltpu.VMEM((2 * X, 1, LANES), F32),
            pltpu.VMEM((8, LANES), F32),
            pltpu.SemaphoreType.DMA,
            pltpu.SemaphoreType.DMA,
            pltpu.SemaphoreType.DMA((Z,)),
            pltpu.SemaphoreType.DMA,
            pltpu.SemaphoreType.DMA((Z,)),
            pltpu.SemaphoreType.DMA,
            pltpu.SemaphoreType.DMA,
            pltpu.SemaphoreType.DMA,
            pltpu.SemaphoreType.DMA,
            pltpu.SemaphoreType.DMA,
            pltpu.SemaphoreType.DMA,
            pltpu.SemaphoreType.DMA,
            pltpu.SemaphoreType.DMA,
            pltpu.SemaphoreType.DMA,
            pltpu.SemaphoreType.DMA,
        ],
        compiler_params=pltpu.CompilerParams(
            collective_id=0, has_side_effects=True, vmem_limit_bytes=48 * 1024 * 1024
        ),
        name="exchange",
    )(owner, grads, factor)


STEP = 8


def update_kernel(owner_ref, back_ref, head_ref, momentum_ref, new_ref, direction_ref, graft):
    lane = lax.broadcasted_iota(jnp.int32, (ROWS, LANES), 1)
    diagonal = lane == lax.broadcasted_iota(jnp.int32, (ROWS, LANES), 0)
    one = lax.broadcasted_iota(jnp.int32, (1, LANES), 1)

    @pl.when(pl.program_id(0) == 0)
    def _():
        totals = jnp.sum(head_ref[...], axis=0)[1:2]
        grad = pltpu.roll(totals, 64, 1)
        graft[...] = jnp.sqrt(grad) / (jnp.sqrt(totals) + 1e-06)

    @pl.loop(0, STEP)
    def _(q):
        b = pl.program_id(0) * STEP + q
        k = owner_ref[0, b]
        ratio = jnp.sum(jnp.where(one == b, graft[...], 0.0), axis=1, keepdims=True)
        top = jnp.broadcast_to(head_ref[k][0:1], (ROWS, LANES))
        top = jnp.sum(jnp.where(diagonal, top, 0.0), axis=1, keepdims=True)
        scale = top * (ratio * (1.0 / (TOP * TOP)))
        words = back_ref[k]
        for h, code in enumerate(((words << 16) >> 16, words >> 16)):
            at = pl.ds(h * HALF, HALF)
            code = code.astype(F32)
            update = code * jnp.abs(code) * scale
            new = 0.9 * momentum_ref[q, :, at] + update
            new_ref[q, :, at] = new
            direction_ref[q, :, at] = (update + 0.9 * new).astype(BF16)


def apply_update(owner, back, head, momentum):
    block = pl.BlockSpec((STEP, ROWS, B), lambda i: (i, 0, 0))
    return pl.pallas_call(
        update_kernel,
        grid=(PAIRS // STEP,),
        out_shape=(
            jax.ShapeDtypeStruct((PAIRS, ROWS, B), F32),
            jax.ShapeDtypeStruct((PAIRS, ROWS, B), BF16),
        ),
        in_specs=[
            pl.BlockSpec(memory_space=pltpu.SMEM),
            pl.BlockSpec(memory_space=pltpu.VMEM),
            pl.BlockSpec(memory_space=pltpu.VMEM),
            block,
        ],
        out_specs=[block, block],
        scratch_shapes=[pltpu.VMEM((1, LANES), F32)],
        compiler_params=pltpu.CompilerParams(vmem_limit_bytes=24 * 1024 * 1024),
        name="update",
    )(owner, back, head, momentum)


def per_device(grads, momentum, root_factors, owner_table):
    factor = root_factors.reshape(Z, Y, 2, ROWS, B)
    back, head = exchange(owner_table, grads[0], factor)
    new_momentum, direction = apply_update(owner_table, back, head, momentum[0])
    return (new_momentum[None], direction[None])


def solution(mesh):
    in_specs = (
        P("mp", None, "dp", None),
        P("mp", None, "dp", None),
        P("mp", "dp", None, None),
        P("mp", None),
    )
    out_specs = (P("mp", None, "dp", None), P("mp", None, "dp", None))
    return jax.shard_map(
        per_device, mesh=mesh, in_specs=in_specs, out_specs=out_specs, check_vma=False
    )
```

time: 214 us -> 77.8 us (0.36)
  blocking collectives: 91.7 us -> 0 us
  Pallas kernels: 0 us -> 75.2 us
  waiting for transfers between devices: 56.8 us -> 0 us
  matrix products: 23.8 us -> 0 us
  starting transfers between devices: 21.1 us -> 0 us
  other arithmetic: 13.2 us -> 0 us
  local copies, waits for them, and re-layouts: 6.37 us -> 1.88 us
    psum x1 -> x0, blocking collectives: 91.7 us -> none  [per_device(): grad_total, pre_total = lax.psum((grad_sq, pre_sq), ('dp', 'mp'))]
    pallas_call x0 -> x2, Pallas kernels: none -> 75.2 us  [the longest x1 70.4 us: exchange(): pl.pallas_call(exchange_kernel, out_shape=(jax.ShapeDtypeStruct((PAIRS, R...]
    all_to_all x2 -> x0, waiting for transfers between devices: 49.7 us -> none  [the longest x1 49.7 us: per_device(): lax.all_to_all(outgoing, 'dp', split_axis=0, concat_axis=0, tiled=True)]
    dot_general x2 -> x0, matrix products: 23.8 us -> none  [matmul_f32(): return jnp.dot(first_matrix, second_matrix, precision=lax.Precision.HIGHEST)]
    all_to_all x2 -> x0, starting transfers between devices: 18.9 us -> none  [the longest x1 13.2 us: per_device(): lax.all_to_all(outgoing, 'dp', split_axis=0, concat_axis=0, tiled=True)]
    ppermute x1 -> x0, waiting for transfers between devices: 7.13 us -> none  [from_partner(): return lax.ppermute(block, axis, route)]
    select_n x6 -> x0, other arithmetic: 6.79 us -> none  [the longest x1 4.55 us: per_device(): left_factor = jnp.where(is_even, own_factor, partner)]
    convert_element_type x2 -> x0, other arithmetic: 5.2 us -> none  [the longest x1 4.61 us: per_device(): direction = (update + 0.9 * new_momentum).astype(jnp.bfloat16)]
  transfers between devices with their start and end apart: 3 -> 0, of which waited for: 2 -> 0; matrix products, arithmetic and copies ran while one was open for 0% -> 0% of each run, Pallas kernels for 0% -> 0%
where the time goes in v1:
time: 77.8 us; the launch traced here: 77.7 us
  Pallas kernels  75.2 us (97%)
  local copies, waits for them, and re-layouts  1.88 us (2%)
    pallas_call x1, Pallas kernels, exchange(): pl.pallas_call(exchange_kernel, out_shape=(jax.ShapeDtypeStruct((PAIRS, R...  70.4 us
    pallas_call x1, Pallas kernels, apply_update(): pl.pallas_call(update_kernel, grid=(PAIRS // STEP,), out_shape=(jax.Shape...  4.73 us
    unnamed x6, local copies, waits for them, and re-layouts  1.88 us

profile of v1, /device:TPU:1, one launch (start us, length us, event | category | flops | bytes accessed | tf_op | source)
XLA Modules:
  0.0 77.7 jit_solution(17728747571539814188)
XLA Ops:
  0.6 0.0 copy-start.1
  0.6 1.2 %copy-done.1 = bf16[1,32,16,1024]{3,2,1,0:T(8,128)(2,1)S(1)} copy-done((bf16[1,32,16,1024]{3,2,1,0:T(8,128)(2,1)S(1)}, bf16[1,32,16,1024]{3,2,1,0:T(8,128)(2,1)}, u32[]{:S(2)}) %copy-start.1) | copy-done | bytes 1048600
  1.9 0.0 copy-start.2
  1.9 0.7 copy-done.2
  2.5 0.0 copy-start
  2.5 70.4 %exchange.1 = (s32[32,16,512]{2,1,0:T(8,128)S(1)}, f32[32,2,128]{2,1,0:T(2,128)S(1)}) custom-call(s32[1,32]{1,0:T(1,128)S(1)} %copy-done.2, bf16[32,16,1024]{2,1,0:T(8,128)(2,1)S(1)} %bitcast.6, f32[8,4,2,16,1024]{4,3,2,1,0:T(8,128)} %bitcast.7), custom_call_target="tpu_custom_call" | custom-call | tf_op jit(solution)/shard_map/exchange/pallas_call | solution.py:290
  72.9 0.0 copy-done
  73.0 4.7 %update.1 = (f32[32,16,1024]{2,1,0:T(8,128)}, bf16[32,16,1024]{2,1,0:T(8,128)(2,1)}) custom-call(s32[1,32]{1,0:T(1,128)S(1)} %copy-done.2, s32[32,16,512]{2,1,0:T(8,128)S(1)} %get-tuple-element.6.back_ref, f32[32,2,128]{2,1,0:T(2,128)S(1)} %get-tuple-element.7.head_ref, f32[32,16,1024]{2,1,0:T(8,128)S(1)} %bitcast.5), custom_call_target="tpu_custom_call" | custom-call | tf_op jit(solution)/shard_map/update/pallas_call | solution.py:371
Async XLA Ops:
  0.6 1.2 %copy-start.1 = (bf16[1,32,16,1024]{3,2,1,0:T(8,128)(2,1)S(1)}, bf16[1,32,16,1024]{3,2,1,0:T(8,128)(2,1)}, u32[]{:S(2)}) copy-start(bf16[1,32,16,1024]{3,2,1,0:T(8,128)(2,1)} %param.4) | copy-start | bytes 3145732
  1.9 0.7 copy-start.2
  2.5 70.4 %copy-start = (f32[1,32,16,1024]{3,2,1,0:T(8,128)S(1)}, f32[1,32,16,1024]{3,2,1,0:T(8,128)}, u32[]{:S(2)}) copy-start(f32[1,32,16,1024]{3,2,1,0:T(8,128)} %param.5) | copy-start | bytes 6291460

commit v2 on v1

--- a/solution.py
+++ b/solution.py
@@ -15,26 +15,34 @@
 MESH = pl.DeviceIdType.MESH
 F32 = jnp.float32
 BF16 = jnp.bfloat16
-OFFSETS = (0, 1, 7, 2, 6, 3, 5, 4)
+OFFSETS = (3, 5, 4, 0, 2, 6, 1, 7)
+OWN = OFFSETS.index(0)
+PACKED = 6
 
 
 def offset_at(i):
-    step = (i + 1) // 2
-    return lax.rem(step + (1 - i % 2) * (8 - 2 * step), 8)
-
-
-def block_of(owner_ref, pair):
-    found = jnp.int32(0)
-    for b in range(PAIRS):
-        found = jnp.where(owner_ref[0, b] == pair, b, found)
+    found = jnp.int32(OFFSETS[0])
+    for n in range(1, Z):
+        found = jnp.where(i == n, OFFSETS[n], found)
     return found
 
 
+def packed_inverse(owner_row):
+    lane = lax.broadcasted_iota(jnp.int32, (1, PAIRS), 1)
+    words = []
+    for w in range((PAIRS + PACKED - 1) // PACKED):
+        at = owner_row - PACKED * w
+        inside = (at >= 0) & (at < PACKED)
+        shift = 5 * jnp.where(inside, at, 0)
+        words.append(jnp.sum(jnp.where(inside, lane << shift, 0)))
+    return words
+
+
 def exchange_kernel(
-    owner_ref, grads_ref, factor_hbm,
+    owner_hbm, grads_hbm, factor_hbm,
     back_ref, head_ref,
-    factor, outgoing, gathered, left, right, left_other, product, coded, heads, sums, seen,
-    factor_sem, grad_send, grad_recv, sib_send, sib_recv, fac_send, fac_recv,
+    owner_rows, grads_ref, inverse, factor, outgoing, gathered, left, right, left_other, product, coded, heads, sums, seen,
+    owner_sem, grads_sem, factor_sem, grad_send, grad_recv, sib_send, sib_recv, fac_send, fac_recv,
     back_send, back_recv, sum_send, sum_recv, head_send, head_recv, local_sem, head_local,
 ):
     me = lax.axis_index("dp")
@@ -46,14 +54,18 @@
     sibling = {"dp": pair * 2 + (1 - c)}
 
     def chip(i, dy):
-        return lax.rem(z + Z - offset_at(i), Z) * Y + lax.rem(y + dy, Y)
+        return lax.rem(z + Z - OFFSETS[i], Z) * Y + lax.rem(y + dy, Y)
+
+    owner_in = pltpu.make_async_copy(owner_hbm, owner_rows, owner_sem)
+    owner_in.start()
+    grads_in = pltpu.make_async_copy(grads_hbm, grads_ref, grads_sem)
+    grads_in.start()
 
     barrier = pltpu.get_barrier_semaphore()
 
-    @pl.loop(1, PAIRS)
-    def _(s):
-        k = chip(s // Y, s % Y)
-        pl.semaphore_signal(barrier, inc=1, device_id={"dp": k * 2 + c}, device_id_type=MESH)
+    partners = [(i, dy) for i in range(Z) for dy in range(Y) if (OFFSETS[i], dy) != (0, 0)]
+    for i, dy in partners:
+        pl.semaphore_signal(barrier, inc=1, device_id={"dp": chip(i, dy) * 2 + c}, device_id_type=MESH)
 
     pl.semaphore_signal(barrier, inc=1, device_id=sibling, device_id_type=MESH)
 
@@ -65,23 +77,25 @@
     factor_in = pltpu.make_async_copy(factor_hbm, factor, factor_sem)
     factor_in.start()
 
-    @pl.loop(0, PAIRS)
-    def _(s):
-        outgoing[s] = grads_ref[block_of(owner_ref, chip(s // Y, s % Y))]
+    owner_in.wait()
+    words = packed_inverse(owner_rows[...])
+    for w, word in enumerate(words):
+        inverse[w] = word
+    grads_in.wait()
+    for k in range(PAIRS):
+        outgoing[k] = grads_ref[(words[k // PACKED] >> (5 * (k % PACKED))) & (PAIRS - 1)]
 
     pl.semaphore_wait(barrier, (PAIRS - 1) + 1 + (2 * X - 2))
 
-    own_rows = pltpu.make_async_copy(outgoing.at[0], gathered.at[0, y, c], local_sem)
+    for i, dy in partners:
+        k = chip(i, dy)
+        pltpu.make_async_remote_copy(
+            src_ref=outgoing.at[k], dst_ref=gathered.at[i, y, c],
+            send_sem=grad_send, recv_sem=grad_recv.at[i],
+            device_id={"dp": k * 2 + c}, device_id_type=MESH,
+        ).start()
+    own_rows = pltpu.make_async_copy(outgoing.at[pair], gathered.at[OWN, y, c], local_sem)
     own_rows.start()
-
-    @pl.loop(1, PAIRS)
-    def _(s):
-        i = s // Y
-        pltpu.make_async_remote_copy(
-            src_ref=outgoing.at[s], dst_ref=gathered.at[i, y, c],
-            send_sem=grad_send, recv_sem=grad_recv.at[i],
-            device_id={"dp": chip(i, s % Y) * 2 + c}, device_id_type=MESH,
-        ).start()
 
     factor_in.wait()
 
@@ -129,23 +143,18 @@
     own_rows.wait()
 
     def pass_on(i):
-        @pl.when(i == 0)
-        def _():
-            whole(gathered.at[0, pl.ds(0, Y - 1), 0], grad_send, grad_recv.at[0]).wait_recv()
-
-        @pl.when(i > 0)
-        def _():
+        if i == OWN:
+            whole(gathered.at[i, pl.ds(0, Y - 1), 0], grad_send, grad_recv.at[i]).wait_recv()
+        else:
             whole(gathered.at[i, :, 0], grad_send, grad_recv.at[i]).wait_recv()
-
         pltpu.make_async_remote_copy(
             src_ref=gathered.at[i, :, c], dst_ref=gathered.at[i, :, c],
             send_sem=sib_send, recv_sem=sib_recv.at[i],
             device_id=sibling, device_id_type=MESH,
         ).start()
 
-    @pl.loop(0, 2)
-    def _(i):
-        pass_on(i)
+    pass_on(0)
+    pass_on(1)
 
     @pl.when(c == 0)
     def _():
@@ -155,27 +164,19 @@
     def _():
         whole(left, fac_send, fac_recv).wait_recv()
 
-    @pl.loop(0, Y)
-    def _(j):
-        @pl.when(j > 0)
-        def _():
+    for j in range(Y):
+        if j > 0:
             pass_on(2 * j)
             pass_on(2 * j + 1)
-
         whole(gathered.at[2 * j, :, 0], sib_send, sib_recv.at[2 * j]).wait_recv()
         whole(gathered.at[2 * j + 1, :, 0], sib_send, sib_recv.at[2 * j + 1]).wait_recv()
-        some = gathered[pl.ds(2 * j, 2)].reshape(2 * LANES, B)
-        cols = pl.ds(pl.multiple_of(j * 2 * LANES, 2 * LANES), 2 * LANES)
-        rows = left[:, :, :, :, cols].reshape(B, 2 * LANES)
+        some = gathered[2 * j:2 * j + 2].reshape(2 * LANES, B)
+        rows = left[:, :, :, :, j * 2 * LANES:(j + 1) * 2 * LANES].reshape(B, 2 * LANES)
         term = jnp.dot(rows, some, preferred_element_type=F32)
         term = term[:HALF] + term[HALF:]
-
-        @pl.when(j == 0)
-        def _():
+        if j == 0:
             product[...] = term
-
-        @pl.when(j > 0)
-        def _():
+        else:
             product[...] += term
 
     seen[...] = jnp.zeros_like(seen)
@@ -219,7 +220,7 @@
             def _():
                 pltpu.make_async_copy(coded.at[s], back_ref.at[pair], local_sem).start()
 
-    block = block_of(owner_ref, pair)
+    block = (inverse[pair // PACKED] >> (5 * (pair % PACKED))) & (PAIRS - 1)
 
     def grad_sum(i, total):
         rows = gathered[i, :, pl.ds(c, 1)].reshape(Y * ROWS, B).astype(F32)
@@ -294,12 +295,15 @@
             jax.ShapeDtypeStruct((PAIRS, 2, LANES), F32),
         ),
         in_specs=[
-            pl.BlockSpec(memory_space=pltpu.SMEM),
-            pl.BlockSpec(memory_space=pltpu.VMEM),
-            pl.BlockSpec(memory_space=pl.ANY),
+            pl.BlockSpec(memory_space=pltpu.HBM),
+            pl.BlockSpec(memory_space=pltpu.HBM),
+            pl.BlockSpec(memory_space=pltpu.HBM),
         ],
         out_specs=[pl.BlockSpec(memory_space=pltpu.VMEM)] * 2,
         scratch_shapes=[
+            pltpu.VMEM((1, PAIRS), jnp.int32),
+            pltpu.VMEM(grads_words, BF16),
+            pltpu.SMEM((PACKED,), jnp.int32),
             pltpu.VMEM((Z, Y, 2, ROWS, B), F32),
             pltpu.VMEM(grads_words, BF16),
             pltpu.VMEM((Z, Y, 2, ROWS, B), BF16),
@@ -313,6 +317,8 @@
             pltpu.VMEM((8, LANES), F32),
             pltpu.SemaphoreType.DMA,
             pltpu.SemaphoreType.DMA,
+            pltpu.SemaphoreType.DMA,
+            pltpu.SemaphoreType.DMA,
             pltpu.SemaphoreType.DMA((Z,)),
             pltpu.SemaphoreType.DMA,
             pltpu.SemaphoreType.DMA((Z,)),
@@ -334,43 +340,46 @@
     )(owner, grads, factor)
 
 
-STEP = 8
-
-
-def update_kernel(owner_ref, back_ref, head_ref, momentum_ref, new_ref, direction_ref, graft):
+STEP = 4
+
+
+def update_kernel(owner_ref, back_ref, head_ref, momentum_ref, new_hbm, direction_hbm, new, direction, scales, sem):
     lane = lax.broadcasted_iota(jnp.int32, (ROWS, LANES), 1)
     diagonal = lane == lax.broadcasted_iota(jnp.int32, (ROWS, LANES), 0)
-    one = lax.broadcasted_iota(jnp.int32, (1, LANES), 1)
-
-    @pl.when(pl.program_id(0) == 0)
-    def _():
-        totals = jnp.sum(head_ref[...], axis=0)[1:2]
-        grad = pltpu.roll(totals, 64, 1)
-        graft[...] = jnp.sqrt(grad) / (jnp.sqrt(totals) + 1e-06)
-
-    @pl.loop(0, STEP)
-    def _(q):
-        b = pl.program_id(0) * STEP + q
+    heads = head_ref[...]
+    totals = jnp.sum(heads, axis=0)[1:2]
+    grad = pltpu.roll(totals, 64, 1)
+    graft = jnp.sqrt(grad) / (jnp.sqrt(totals) + 1e-06) * (1.0 / (TOP * TOP))
+    for k in range(PAIRS):
+        top = jnp.broadcast_to(heads[k, 0:1], (ROWS, LANES))
+        top = jnp.sum(jnp.where(diagonal, top, 0.0), axis=1, keepdims=True)
+        scales[k] = jnp.broadcast_to(top, (ROWS, LANES))
+    copies = []
+    for b in range(PAIRS):
         k = owner_ref[0, b]
-        ratio = jnp.sum(jnp.where(one == b, graft[...], 0.0), axis=1, keepdims=True)
-        top = jnp.broadcast_to(head_ref[k][0:1], (ROWS, LANES))
-        top = jnp.sum(jnp.where(diagonal, top, 0.0), axis=1, keepdims=True)
-        scale = top * (ratio * (1.0 / (TOP * TOP)))
+        scale = scales[k] * jnp.broadcast_to(graft[:, b:b + 1], (ROWS, LANES))
         words = back_ref[k]
         for h, code in enumerate(((words << 16) >> 16, words >> 16)):
-            at = pl.ds(h * HALF, HALF)
             code = code.astype(F32)
-            update = code * jnp.abs(code) * scale
-            new = 0.9 * momentum_ref[q, :, at] + update
-            new_ref[q, :, at] = new
-            direction_ref[q, :, at] = (update + 0.9 * new).astype(BF16)
+            code = code * jnp.abs(code)
+            for q in range(HALF // LANES):
+                at = slice(h * HALF + q * LANES, h * HALF + (q + 1) * LANES)
+                update = code[:, q * LANES:(q + 1) * LANES] * scale
+                fresh = 0.9 * momentum_ref[b, :, at] + update
+                new[b, :, at] = fresh
+                direction[b, :, at] = (update + 0.9 * fresh).astype(BF16)
+        if (b + 1) % STEP == 0:
+            part = pl.ds(b + 1 - STEP, STEP)
+            for n, (have, give) in enumerate(((new, new_hbm), (direction, direction_hbm))):
+                copies.append(pltpu.make_async_copy(have.at[part], give.at[part], sem.at[n, b // STEP]))
+                copies[-1].start()
+    for copy in copies:
+        copy.wait()
 
 
 def apply_update(owner, back, head, momentum):
-    block = pl.BlockSpec((STEP, ROWS, B), lambda i: (i, 0, 0))
     return pl.pallas_call(
         update_kernel,
-        grid=(PAIRS // STEP,),
         out_shape=(
             jax.ShapeDtypeStruct((PAIRS, ROWS, B), F32),
             jax.ShapeDtypeStruct((PAIRS, ROWS, B), BF16),
@@ -379,10 +388,15 @@
             pl.BlockSpec(memory_space=pltpu.SMEM),
             pl.BlockSpec(memory_space=pltpu.VMEM),
             pl.BlockSpec(memory_space=pltpu.VMEM),
-            block,
+            pl.BlockSpec(memory_space=pltpu.VMEM),
         ],
-        out_specs=[block, block],
-        scratch_shapes=[pltpu.VMEM((1, LANES), F32)],
+        out_specs=[pl.BlockSpec(memory_space=pltpu.HBM)] * 2,
+        scratch_shapes=[
+            pltpu.VMEM((PAIRS, ROWS, B), F32),
+            pltpu.VMEM((PAIRS, ROWS, B), BF16),
+            pltpu.VMEM((PAIRS, ROWS, LANES), F32),
+            pltpu.SemaphoreType.DMA((2, PAIRS // STEP)),
+        ],
         compiler_params=pltpu.CompilerParams(vmem_limit_bytes=24 * 1024 * 1024),
         name="update",
     )(owner, back, head, momentum)

time: 77.8 us -> 73.2 us (0.941)
  Pallas kernels: 75.2 us -> 70.5 us
    pallas_call x1, Pallas kernels: 70.4 us -> 67.4 us  [exchange(): pl.pallas_call(exchange_kernel, out_shape=(jax.ShapeDtypeStruct((PAIRS, R...]
    pallas_call x1, Pallas kernels: 4.73 us -> 3.06 us  [apply_update(): pl.pallas_call(update_kernel, out_shape=(jax.ShapeDtypeStruct((PAIRS, ROW...]
where the time goes in v2:
time: 73.2 us; the launch traced here: 73 us
  Pallas kernels  70.5 us (96%)
  local copies, waits for them, and re-layouts  1.88 us (3%)
    pallas_call x1, Pallas kernels, exchange(): pl.pallas_call(exchange_kernel, out_shape=(jax.ShapeDtypeStruct((PAIRS, R...  67.4 us
    pallas_call x1, Pallas kernels, apply_update(): pl.pallas_call(update_kernel, out_shape=(jax.ShapeDtypeStruct((PAIRS, ROW...  3.06 us
    unnamed x6, local copies, waits for them, and re-layouts  1.88 us

profile of v2, /device:TPU:1, one launch (start us, length us, event | category | flops | bytes accessed | tf_op | source)
XLA Modules:
  0.0 73.0 jit_solution(15992224128492805213)
XLA Ops:
  0.6 0.0 copy-start.1
  0.6 1.2 %copy-done.1 = bf16[1,32,16,1024]{3,2,1,0:T(8,128)(2,1)S(1)} copy-done((bf16[1,32,16,1024]{3,2,1,0:T(8,128)(2,1)S(1)}, bf16[1,32,16,1024]{3,2,1,0:T(8,128)(2,1)}, u32[]{:S(2)}) %copy-start.1) | copy-done | bytes 1048600
  1.9 0.0 copy-start.2
  1.9 0.7 copy-done.2
  2.5 0.0 copy-start
  2.5 67.4 %exchange.1 = (s32[32,16,512]{2,1,0:T(8,128)S(1)}, f32[32,2,128]{2,1,0:T(2,128)S(1)}) custom-call(s32[1,32]{1,0:T(1,128)S(1)} %copy-done.2, bf16[32,16,1024]{2,1,0:T(8,128)(2,1)S(1)} %bitcast.6, f32[8,4,2,16,1024]{4,3,2,1,0:T(8,128)} %bitcast.7), custom_call_target="tpu_custom_call" | custom-call | tf_op jit(solution)/shard_map/exchange/pallas_call | solution.py:291
  70.0 0.0 copy-done
  70.0 3.1 %update.1 = (f32[32,16,1024]{2,1,0:T(8,128)}, bf16[32,16,1024]{2,1,0:T(8,128)(2,1)}) custom-call(s32[1,32]{1,0:T(1,128)S(1)} %copy-done.2, s32[32,16,512]{2,1,0:T(8,128)S(1)} %get-tuple-element.6.back_ref, f32[32,2,128]{2,1,0:T(2,128)S(1)} %get-tuple-element.7.head_ref, f32[32,16,1024]{2,1,0:T(8,128)S(1)} %bitcast.5), custom_call_target="tpu_custom_call" | custom-call | tf_op jit(solution)/shard_map/update/pallas_call | solution.py:381
Async XLA Ops:
  0.6 1.2 %copy-start.1 = (bf16[1,32,16,1024]{3,2,1,0:T(8,128)(2,1)S(1)}, bf16[1,32,16,1024]{3,2,1,0:T(8,128)(2,1)}, u32[]{:S(2)}) copy-start(bf16[1,32,16,1024]{3,2,1,0:T(8,128)(2,1)} %param.4) | copy-start | bytes 3145732
  1.9 0.7 copy-start.2
  2.5 67.5 %copy-start = (f32[1,32,16,1024]{3,2,1,0:T(8,128)S(1)}, f32[1,32,16,1024]{3,2,1,0:T(8,128)}, u32[]{:S(2)}) copy-start(f32[1,32,16,1024]{3,2,1,0:T(8,128)} %param.5) | copy-start | bytes 6291460

commit v3 on v2

--- a/solution.py
+++ b/solution.py
@@ -18,6 +18,7 @@
 OFFSETS = (3, 5, 4, 0, 2, 6, 1, 7)
 OWN = OFFSETS.index(0)
 PACKED = 6
+HELD = PAIRS - 2 * Y
 
 
 def offset_at(i):
@@ -39,10 +40,10 @@
 
 
 def exchange_kernel(
-    owner_hbm, grads_hbm, factor_hbm,
+    owner_rows, grads_hbm, factor_hbm,
     back_ref, head_ref,
-    owner_rows, grads_ref, inverse, factor, outgoing, gathered, left, right, left_other, product, coded, heads, sums, seen,
-    owner_sem, grads_sem, factor_sem, grad_send, grad_recv, sib_send, sib_recv, fac_send, fac_recv,
+    grads_ref, inverse, factor, outgoing, gathered, left, right, left_other, product, coded, heads, sums, seen,
+    grads_sem, factor_sem, grad_send, grad_recv, sib_send, sib_recv, fac_send, fac_recv,
     back_send, back_recv, sum_send, sum_recv, head_send, head_recv, local_sem, head_local,
 ):
     me = lax.axis_index("dp")
@@ -56,8 +57,6 @@
     def chip(i, dy):
         return lax.rem(z + Z - OFFSETS[i], Z) * Y + lax.rem(y + dy, Y)
 
-    owner_in = pltpu.make_async_copy(owner_hbm, owner_rows, owner_sem)
-    owner_in.start()
     grads_in = pltpu.make_async_copy(grads_hbm, grads_ref, grads_sem)
     grads_in.start()
 
@@ -77,7 +76,6 @@
     factor_in = pltpu.make_async_copy(factor_hbm, factor, factor_sem)
     factor_in.start()
 
-    owner_in.wait()
     words = packed_inverse(owner_rows[...])
     for w, word in enumerate(words):
         inverse[w] = word
@@ -91,7 +89,7 @@
         k = chip(i, dy)
         pltpu.make_async_remote_copy(
             src_ref=outgoing.at[k], dst_ref=gathered.at[i, y, c],
-            send_sem=grad_send, recv_sem=grad_recv.at[i],
+            send_sem=grad_send, recv_sem=grad_recv.at[i, y],
             device_id={"dp": k * 2 + c}, device_id_type=MESH,
         ).start()
     own_rows = pltpu.make_async_copy(outgoing.at[pair], gathered.at[OWN, y, c], local_sem)
@@ -142,19 +140,30 @@
 
     own_rows.wait()
 
-    def pass_on(i):
-        if i == OWN:
-            whole(gathered.at[i, pl.ds(0, Y - 1), 0], grad_send, grad_recv.at[i]).wait_recv()
-        else:
-            whole(gathered.at[i, :, 0], grad_send, grad_recv.at[i]).wait_recv()
+    def arrived(i, dy):
+        if (OFFSETS[i], dy) != (0, 0):
+            q = lax.rem(y + dy, Y)
+            whole(gathered.at[i, q, 0], grad_send, grad_recv.at[i, q]).wait_recv()
+
+    def pass_on(part, i):
         pltpu.make_async_remote_copy(
-            src_ref=gathered.at[i, :, c], dst_ref=gathered.at[i, :, c],
-            send_sem=sib_send, recv_sem=sib_recv.at[i],
+            src_ref=part, dst_ref=part, send_sem=sib_send, recv_sem=sib_recv.at[i],
             device_id=sibling, device_id_type=MESH,
         ).start()
 
-    pass_on(0)
-    pass_on(1)
+    def pass_on_two(j):
+        if j < Y - 1:
+            for i in (2 * j, 2 * j + 1):
+                for dy in range(Y):
+                    arrived(i, dy)
+                pass_on(gathered.at[i, :, c], i)
+        else:
+            for dy in (0, 1, 3, 2):
+                for i in (2 * j, 2 * j + 1):
+                    arrived(i, dy)
+                    pass_on(gathered.at[i, lax.rem(y + dy, Y), c], i)
+
+    pass_on_two(0)
 
     @pl.when(c == 0)
     def _():
@@ -166,8 +175,7 @@
 
     for j in range(Y):
         if j > 0:
-            pass_on(2 * j)
-            pass_on(2 * j + 1)
+            pass_on_two(j)
         whole(gathered.at[2 * j, :, 0], sib_send, sib_recv.at[2 * j]).wait_recv()
         whole(gathered.at[2 * j + 1, :, 0], sib_send, sib_recv.at[2 * j + 1]).wait_recv()
         some = gathered[2 * j:2 * j + 2].reshape(2 * LANES, B)
@@ -182,6 +190,24 @@
     seen[...] = jnp.zeros_like(seen)
     lane = lax.broadcasted_iota(jnp.int32, (ROWS, LANES), 1)
     diagonal = lane == lax.broadcasted_iota(jnp.int32, (ROWS, LANES), 0)
+
+    def partner(s):
+        return lax.rem(z + offset_at(s // Y), Z) * Y + s % Y
+
+    def give_back(s):
+        k = partner(s)
+
+        @pl.when(k != pair)
+        def _():
+            pltpu.make_async_remote_copy(
+                src_ref=coded.at[s], dst_ref=back_ref.at[pair],
+                send_sem=back_send, recv_sem=back_recv,
+                device_id={"dp": k * 2 + c}, device_id_type=MESH,
+            ).start()
+
+        @pl.when(k == pair)
+        def _():
+            pltpu.make_async_copy(coded.at[s], back_ref.at[pair], local_sem).start()
 
     @pl.loop(0, Y)
     def _(j):
@@ -205,20 +231,10 @@
             code = (jnp.sqrt(size * (1.0 / top)) * TOP + 0.5).astype(jnp.int32)
             code = jnp.where(value < 0.0, -code, code)
             coded[s] = (code[:, :HALF] & 0xFFFF) | (code[:, HALF:] << 16)
-            i = s // Y
-            k = lax.rem(z + offset_at(i), Z) * Y + s % Y
-
-            @pl.when(k != pair)
+
+            @pl.when(s < HELD)
             def _():
-                pltpu.make_async_remote_copy(
-                    src_ref=coded.at[s], dst_ref=back_ref.at[pair],
-                    send_sem=back_send, recv_sem=back_recv,
-                    device_id={"dp": k * 2 + c}, device_id_type=MESH,
-                ).start()
-
-            @pl.when(k == pair)
-            def _():
-                pltpu.make_async_copy(coded.at[s], back_ref.at[pair], local_sem).start()
+                give_back(s)
 
     block = (inverse[pair // PACKED] >> (5 * (pair % PACKED))) & (PAIRS - 1)
 
@@ -246,7 +262,7 @@
     @pl.loop(0, PAIRS)
     def _(s):
         heads[s, 1:2] = total
-        k = lax.rem(z + offset_at(s // Y), Z) * Y + s % Y
+        k = partner(s)
 
         @pl.when(k != pair)
         def _():
@@ -260,8 +276,12 @@
         def _():
             pltpu.make_async_copy(heads.at[s], head_ref.at[pair], head_local).start()
 
+    @pl.loop(HELD, PAIRS)
+    def _(s):
+        give_back(s)
+
     others = pl.ds(0, PAIRS - 1)
-    whole(outgoing.at[others], grad_send, grad_recv.at[0]).wait_send()
+    whole(outgoing.at[others], grad_send, grad_recv.at[0, 0]).wait_send()
     whole(gathered.at[:, :, 0], sib_send, sib_recv.at[0]).wait_send()
 
     @pl.when(c == 0)
@@ -295,13 +315,12 @@
             jax.ShapeDtypeStruct((PAIRS, 2, LANES), F32),
         ),
         in_specs=[
-            pl.BlockSpec(memory_space=pltpu.HBM),
+            pl.BlockSpec(memory_space=pltpu.VMEM),
             pl.BlockSpec(memory_space=pltpu.HBM),
             pl.BlockSpec(memory_space=pltpu.HBM),
         ],
         out_specs=[pl.BlockSpec(memory_space=pltpu.VMEM)] * 2,
         scratch_shapes=[
-            pltpu.VMEM((1, PAIRS), jnp.int32),
             pltpu.VMEM(grads_words, BF16),
             pltpu.SMEM((PACKED,), jnp.int32),
             pltpu.VMEM((Z, Y, 2, ROWS, B), F32),
@@ -318,8 +337,7 @@
             pltpu.SemaphoreType.DMA,
             pltpu.SemaphoreType.DMA,
             pltpu.SemaphoreType.DMA,
-            pltpu.SemaphoreType.DMA,
-            pltpu.SemaphoreType.DMA((Z,)),
+            pltpu.SemaphoreType.DMA((Z, Y)),
             pltpu.SemaphoreType.DMA,
             pltpu.SemaphoreType.DMA((Z,)),
             pltpu.SemaphoreType.DMA,
@@ -334,7 +352,7 @@
             pltpu.SemaphoreType.DMA,
         ],
         compiler_params=pltpu.CompilerParams(
-            collective_id=0, has_side_effects=True, vmem_limit_bytes=48 * 1024 * 1024
+            collective_id=0, has_side_effects=True, vmem_limit_bytes=52 * 1024 * 1024
         ),
         name="exchange",
     )(owner, grads, factor)
@@ -343,7 +361,9 @@
 STEP = 4
 
 
-def update_kernel(owner_ref, back_ref, head_ref, momentum_ref, new_hbm, direction_hbm, new, direction, scales, sem):
+def update_kernel(owner_in, back_ref, head_ref, momentum_ref, new_hbm, direction_hbm, owner_ref, new, direction, scales, owner_sem, sem):
+    owner = pltpu.make_async_copy(owner_in, owner_ref, owner_sem)
+    owner.start()
     lane = lax.broadcasted_iota(jnp.int32, (ROWS, LANES), 1)
     diagonal = lane == lax.broadcasted_iota(jnp.int32, (ROWS, LANES), 0)
     heads = head_ref[...]
@@ -354,6 +374,7 @@
         top = jnp.broadcast_to(heads[k, 0:1], (ROWS, LANES))
         top = jnp.sum(jnp.where(diagonal, top, 0.0), axis=1, keepdims=True)
         scales[k] = jnp.broadcast_to(top, (ROWS, LANES))
+    owner.wait()
     copies = []
     for b in range(PAIRS):
         k = owner_ref[0, b]
@@ -385,16 +406,18 @@
             jax.ShapeDtypeStruct((PAIRS, ROWS, B), BF16),
         ),
         in_specs=[
-            pl.BlockSpec(memory_space=pltpu.SMEM),
+            pl.BlockSpec(memory_space=pl.ANY),
             pl.BlockSpec(memory_space=pltpu.VMEM),
             pl.BlockSpec(memory_space=pltpu.VMEM),
             pl.BlockSpec(memory_space=pltpu.VMEM),
         ],
         out_specs=[pl.BlockSpec(memory_space=pltpu.HBM)] * 2,
         scratch_shapes=[
+            pltpu.SMEM((1, PAIRS), jnp.int32),
             pltpu.VMEM((PAIRS, ROWS, B), F32),
             pltpu.VMEM((PAIRS, ROWS, B), BF16),
             pltpu.VMEM((PAIRS, ROWS, LANES), F32),
+            pltpu.SemaphoreType.DMA,
             pltpu.SemaphoreType.DMA((2, PAIRS // STEP)),
         ],
         compiler_params=pltpu.CompilerParams(vmem_limit_bytes=24 * 1024 * 1024),

time: 73.2 us -> 69.9 us (0.955)
  Pallas kernels: 70.5 us -> 68.5 us
  local copies, waits for them, and re-layouts: 1.88 us -> 0.65 us
    pallas_call x1, Pallas kernels: 67.4 us -> 66 us  [exchange(): pl.pallas_call(exchange_kernel, out_shape=(jax.ShapeDtypeStruct((PAIRS, R...]
    unnamed x6 -> x4, local copies, waits for them, and re-layouts: 1.88 us -> 0.65 us
where the time goes in v3:
time: 69.9 us; the launch traced here: 69.8 us
  Pallas kernels  68.5 us (98%)
    pallas_call x1, Pallas kernels, exchange(): pl.pallas_call(exchange_kernel, out_shape=(jax.ShapeDtypeStruct((PAIRS, R...  66 us
    pallas_call x1, Pallas kernels, apply_update(): pl.pallas_call(update_kernel, out_shape=(jax.ShapeDtypeStruct((PAIRS, ROW...  2.49 us

profile of v3, /device:TPU:1, one launch (start us, length us, event | category | flops | bytes accessed | tf_op | source)
XLA Modules:
  0.0 69.8 jit_solution(7319581331439909515)
XLA Ops:
  0.6 0.0 copy-start.1
  0.6 0.6 copy-done.1
  1.3 0.0 copy-start
  1.3 66.0 %exchange.1 = (s32[32,16,512]{2,1,0:T(8,128)S(1)}, f32[32,2,128]{2,1,0:T(2,128)S(1)}) custom-call(s32[1,32]{1,0:T(1,128)S(1)} %copy-done.1, bf16[32,16,1024]{2,1,0:T(8,128)(2,1)} %bitcast.7, f32[8,4,2,16,1024]{4,3,2,1,0:T(8,128)} %bitcast.6), custom_call_target="tpu_custom_call" | custom-call | tf_op jit(solution)/shard_map/exchange/pallas_call | solution.py:311
  67.3 0.0 copy-done
  67.3 2.5 %update.1 = (f32[32,16,1024]{2,1,0:T(8,128)}, bf16[32,16,1024]{2,1,0:T(8,128)(2,1)}) custom-call(s32[1,32]{1,0:T(1,128)S(1)} %copy-done.1, s32[32,16,512]{2,1,0:T(8,128)S(1)} %get-tuple-element.6.back_ref, f32[32,2,128]{2,1,0:T(2,128)S(1)} %get-tuple-element.7.head_ref, f32[32,16,1024]{2,1,0:T(8,128)S(1)} %bitcast.5), custom_call_target="tpu_custom_call" | custom-call | tf_op jit(solution)/shard_map/update/pallas_call | solution.py:402
Async XLA Ops:
  0.6 0.7 copy-start.1
  1.3 66.0 %copy-start = (f32[1,32,16,1024]{3,2,1,0:T(8,128)S(1)}, f32[1,32,16,1024]{3,2,1,0:T(8,128)}, u32[]{:S(2)}) copy-start(f32[1,32,16,1024]{3,2,1,0:T(8,128)} %param.5) | copy-start | bytes 6291460

commit v4 on v3

--- a/solution.py
+++ b/solution.py
@@ -15,7 +15,7 @@
 MESH = pl.DeviceIdType.MESH
 F32 = jnp.float32
 BF16 = jnp.bfloat16
-OFFSETS = (3, 5, 4, 0, 2, 6, 1, 7)
+OFFSETS = (4, 0, 2, 6, 3, 5, 1, 7)
 OWN = OFFSETS.index(0)
 PACKED = 6
 HELD = PAIRS - 2 * Y
@@ -85,13 +85,23 @@
 
     pl.semaphore_wait(barrier, (PAIRS - 1) + 1 + (2 * X - 2))
 
-    for i, dy in partners:
-        k = chip(i, dy)
-        pltpu.make_async_remote_copy(
-            src_ref=outgoing.at[k], dst_ref=gathered.at[i, y, c],
-            send_sem=grad_send, recv_sem=grad_recv.at[i, y],
-            device_id={"dp": k * 2 + c}, device_id_type=MESH,
-        ).start()
+    def send_rows(first):
+        early = [p for p in partners if (OFFSETS[p[0]] + (1) * p[1] + first) % 2 == 0]
+        late = [p for p in partners if p not in early]
+        for i, dy in early + late:
+            k = chip(i, dy)
+            pltpu.make_async_remote_copy(
+                src_ref=outgoing.at[k], dst_ref=gathered.at[i, y, c],
+                send_sem=grad_send, recv_sem=grad_recv.at[i, y],
+                device_id={"dp": k * 2 + c}, device_id_type=MESH,
+            ).start()
+
+    colour = (z + 1 * y) % 2
+    for first in range(2):
+        @pl.when(colour == first)
+        def _(first=first):
+            send_rows(first)
+
     own_rows = pltpu.make_async_copy(outgoing.at[pair], gathered.at[OWN, y, c], local_sem)
     own_rows.start()
 

time: 69.9 us -> 64.7 us (0.926)
  Pallas kernels: 68.5 us -> 62.9 us
    pallas_call x1, Pallas kernels: 66 us -> 60.4 us  [exchange(): pl.pallas_call(exchange_kernel, out_shape=(jax.ShapeDtypeStruct((PAIRS, R...]
where the time goes in v4:
time: 64.7 us; the launch traced here: 64.2 us
  Pallas kernels  62.9 us (97%)
  between operations  0.66 us (1%)
  local copies, waits for them, and re-layouts  0.65 us (1%)
    pallas_call x1, Pallas kernels, exchange(): pl.pallas_call(exchange_kernel, out_shape=(jax.ShapeDtypeStruct((PAIRS, R...  60.4 us
    pallas_call x1, Pallas kernels, apply_update(): pl.pallas_call(update_kernel, out_shape=(jax.ShapeDtypeStruct((PAIRS, ROW...  2.49 us

profile of v4, /device:TPU:1, one launch (start us, length us, event | category | flops | bytes accessed | tf_op | source)
XLA Modules:
  0.0 64.2 jit_solution(12014812733728881396)
XLA Ops:
  0.6 0.0 copy-start.1
  0.6 0.6 %copy-done.1 = s32[1,32]{1,0:T(1,128)S(1)} copy-done((s32[1,32]{1,0:T(1,128)S(1)}, s32[1,32]{1,0:T(1,128)}, u32[]{:S(2)}) %copy-start.1) | copy-done | bytes 152
  1.3 0.0 copy-start
  1.3 60.4 %exchange.1 = (s32[32,16,512]{2,1,0:T(8,128)S(1)}, f32[32,2,128]{2,1,0:T(2,128)S(1)}) custom-call(s32[1,32]{1,0:T(1,128)S(1)} %copy-done.1, bf16[32,16,1024]{2,1,0:T(8,128)(2,1)} %bitcast.7, f32[8,4,2,16,1024]{4,3,2,1,0:T(8,128)} %bitcast.6), custom_call_target="tpu_custom_call" | custom-call | tf_op jit(solution)/shard_map/exchange/pallas_call | solution.py:321
  61.7 0.0 copy-done
  61.8 2.5 %update.1 = (f32[32,16,1024]{2,1,0:T(8,128)}, bf16[32,16,1024]{2,1,0:T(8,128)(2,1)}) custom-call(s32[1,32]{1,0:T(1,128)S(1)} %copy-done.1, s32[32,16,512]{2,1,0:T(8,128)S(1)} %get-tuple-element.6.back_ref, f32[32,2,128]{2,1,0:T(2,128)S(1)} %get-tuple-element.7.head_ref, f32[32,16,1024]{2,1,0:T(8,128)S(1)} %bitcast.5), custom_call_target="tpu_custom_call" | custom-call | tf_op jit(solution)/shard_map/update/pallas_call | solution.py:412
Async XLA Ops:
  0.6 0.7 %copy-start.1 = (s32[1,32]{1,0:T(1,128)S(1)}, s32[1,32]{1,0:T(1,128)}, u32[]{:S(2)}) copy-start(s32[1,32]{1,0:T(1,128)} %owner_in.1) | copy-start | bytes 388
  1.3 60.5 %copy-start = (f32[1,32,16,1024]{3,2,1,0:T(8,128)S(1)}, f32[1,32,16,1024]{3,2,1,0:T(8,128)}, u32[]{:S(2)}) copy-start(f32[1,32,16,1024]{3,2,1,0:T(8,128)} %param.5) | copy-start | bytes 6291460

commit v5 on v4

--- a/solution.py
+++ b/solution.py
@@ -18,7 +18,8 @@
 OFFSETS = (4, 0, 2, 6, 3, 5, 1, 7)
 OWN = OFFSETS.index(0)
 PACKED = 6
-HELD = PAIRS - 2 * Y
+HELD = PAIRS - 9
+CHUNKS = (128, 128, 128, 128)
 
 
 def offset_at(i):
@@ -41,9 +42,9 @@
 
 def exchange_kernel(
     owner_rows, grads_hbm, factor_hbm,
-    back_ref, head_ref,
-    grads_ref, inverse, factor, outgoing, gathered, left, right, left_other, product, coded, heads, sums, seen,
-    grads_sem, factor_sem, grad_send, grad_recv, sib_send, sib_recv, fac_send, fac_recv,
+    rows_ref, scale_ref, sums_ref,
+    owner_ref, back_ref, head_ref, grads_ref, inverse, factor, outgoing, gathered, left, right, left_other, product, coded, heads, sums, grad_seen,
+    owner_sem, grads_sem, factor_sem, grad_send, grad_recv, sib_send, sib_recv, fac_send, fac_recv,
     back_send, back_recv, sum_send, sum_recv, head_send, head_recv, local_sem, head_local,
 ):
     me = lax.axis_index("dp")
@@ -57,6 +58,8 @@
     def chip(i, dy):
         return lax.rem(z + Z - OFFSETS[i], Z) * Y + lax.rem(y + dy, Y)
 
+    owner_in = pltpu.make_async_copy(owner_rows, owner_ref, owner_sem)
+    owner_in.start()
     grads_in = pltpu.make_async_copy(grads_hbm, grads_ref, grads_sem)
     grads_in.start()
 
@@ -85,10 +88,13 @@
 
     pl.semaphore_wait(barrier, (PAIRS - 1) + 1 + (2 * X - 2))
 
+    def by_turn(p):
+        return (p[0] // 2, p[1], p[0])
+
     def send_rows(first):
         early = [p for p in partners if (OFFSETS[p[0]] + (1) * p[1] + first) % 2 == 0]
         late = [p for p in partners if p not in early]
-        for i, dy in early + late:
+        for i, dy in sorted(early, key=by_turn) + sorted(late, key=by_turn):
             k = chip(i, dy)
             pltpu.make_async_remote_copy(
                 src_ref=outgoing.at[k], dst_ref=gathered.at[i, y, c],
@@ -196,99 +202,93 @@
             product[...] = term
         else:
             product[...] += term
-
-    seen[...] = jnp.zeros_like(seen)
+        own = gathered[2 * j:2 * j + 2, :, pl.ds(c, 1)].reshape(2 * Y * ROWS, B).astype(F32)
+        squares = _fold(own * own)
+        if j == 0:
+            grad_seen[...] = squares
+        else:
+            grad_seen[...] += squares
+
     lane = lax.broadcasted_iota(jnp.int32, (ROWS, LANES), 1)
-    diagonal = lane == lax.broadcasted_iota(jnp.int32, (ROWS, LANES), 0)
-
-    def partner(s):
-        return lax.rem(z + offset_at(s // Y), Z) * Y + s % Y
-
-    def give_back(s):
-        k = partner(s)
-
-        @pl.when(k != pair)
-        def _():
+    diagonal = lane == lax.broadcasted_iota(jnp.int32, (ROWS, LANES), 0) + 2 * PAIRS
+
+    def send_back(source, sent, landed, at_home, n):
+        i, turn = n // (2 * Y) * 2 + n % 2, n % (2 * Y) // 2
+        q = lax.rem(y + turn, Y)
+        s = i * Y + q
+        k = lax.rem(z + OFFSETS[i], Z) * Y + q
+        if (i, turn) == (OWN, 0):
+            pltpu.make_async_copy(source.at[s], landed.at[pair], at_home).start()
+        else:
             pltpu.make_async_remote_copy(
-                src_ref=coded.at[s], dst_ref=back_ref.at[pair],
-                send_sem=back_send, recv_sem=back_recv,
+                src_ref=source.at[s], dst_ref=landed.at[pair],
+                send_sem=sent[0], recv_sem=sent[1],
                 device_id={"dp": k * 2 + c}, device_id_type=MESH,
             ).start()
 
-        @pl.when(k == pair)
-        def _():
-            pltpu.make_async_copy(coded.at[s], back_ref.at[pair], local_sem).start()
-
-    @pl.loop(0, Y)
-    def _(j):
-        base = pl.multiple_of(j * LANES, LANES)
-        rows = product[pl.ds(base, LANES)]
-        high = rows.astype(BF16)
-        low = (rows - high.astype(F32)).astype(BF16)
+    def give_back(n):
+        send_back(coded, (back_send, back_recv), back_ref, local_sem, n)
+
+    def encode(s):
+        value = product[pl.ds(pl.multiple_of(s * ROWS, ROWS), ROWS)]
+        size = jnp.abs(value)
+        top = jnp.maximum(jnp.max(size, axis=1, keepdims=True), 1e-37)
+        heads[s] = jnp.sum(jnp.where(diagonal, jnp.broadcast_to(top, (ROWS, LANES)), 0.0), axis=0, keepdims=True)
+        code = (jnp.sqrt(size * (1.0 / top)) * TOP + 0.5).astype(jnp.int32)
+        code = jnp.where(value < 0.0, -code, code)
+        coded[s] = (code[:, :HALF] & 0xFFFF) | (code[:, HALF:] << 16)
+
+    def multiply(start, rows):
+        part = product[start:start + rows]
+        high = part.astype(BF16)
+        low = (part - high.astype(F32)).astype(BF16)
         both = jnp.concatenate([high, low], axis=0)
         by_high = jnp.dot(both, right[0].reshape(B, B), preferred_element_type=F32)
         by_low = jnp.dot(high, right[1].reshape(B, B), preferred_element_type=F32)
-        product[pl.ds(base, LANES)] = by_high[:LANES] + (by_high[LANES:] + by_low)
-
-        @pl.loop(0, 2 * Y)
+        value = by_high[:rows] + (by_high[rows:] + by_low)
+        product[start:start + rows] = value
+        return _fold(value * value)
+
+    def encode_all(start, rows):
+        @pl.loop(0, rows // ROWS, unroll=4)
         def _(q):
-            s = j * 2 * Y + q
-            value = product[pl.ds(pl.multiple_of(s * ROWS, ROWS), ROWS)]
-            seen[...] += _fold(value * value)
-            size = jnp.abs(value)
-            top = jnp.maximum(jnp.max(size, axis=1, keepdims=True), 1e-37)
-            heads[s, 0:1] = jnp.sum(jnp.where(diagonal, jnp.broadcast_to(top, (ROWS, LANES)), 0.0), axis=0, keepdims=True)
-            code = (jnp.sqrt(size * (1.0 / top)) * TOP + 0.5).astype(jnp.int32)
-            code = jnp.where(value < 0.0, -code, code)
-            coded[s] = (code[:, :HALF] & 0xFFFF) | (code[:, HALF:] << 16)
-
-            @pl.when(s < HELD)
-            def _():
-                give_back(s)
+            encode(start // ROWS + q)
+
+    done = 0
+    pre_tile = jnp.zeros((8, LANES), F32)
+    for rows in CHUNKS:
+        pre_tile = pre_tile + multiply(done, rows)
+        if done + rows < HALF:
+            encode_all(done, rows)
+            for n in range(done // ROWS, min((done + rows) // ROWS, HELD)):
+                give_back(n)
+            done += rows
+
+    owner_in.wait()
 
     block = (inverse[pair // PACKED] >> (5 * (pair % PACKED))) & (PAIRS - 1)
-
-    def grad_sum(i, total):
-        rows = gathered[i, :, pl.ds(c, 1)].reshape(Y * ROWS, B).astype(F32)
-        return total + _fold(rows * rows)
-
-    grad_sq = jnp.sum(lax.fori_loop(0, Z, grad_sum, jnp.zeros((8, LANES), F32)))
-    pre_sq = jnp.sum(seen[...])
+    grad_sq = jnp.sum(grad_seen[...])
+    pre_sq = jnp.sum(pre_tile)
     one = lax.broadcasted_iota(jnp.int32, (1, LANES), 1)
-    sums[0] = jnp.where(one == block, pre_sq, 0.0) + jnp.where(one == block + 64, grad_sq, 0.0)
-
-    @pl.loop(1, 2 * X)
-    def _(s):
+    sums[0] = jnp.where(one == block, pre_sq, 0.0) + jnp.where(one == block + PAIRS, grad_sq, 0.0)
+    for s in range(1, 2 * X):
         target = {"dp": pair * 2 + lax.rem(c + s, 2), "mp": lax.rem(x + s // 2, X)}
         pltpu.make_async_remote_copy(
             src_ref=sums.at[0], dst_ref=sums.at[s],
             send_sem=sum_send, recv_sem=sum_recv,
             device_id=target, device_id_type=MESH,
         ).start()
-
+    encode_all(done, HALF - done)
+    for n in range(done // ROWS, HELD):
+        give_back(n)
     whole(sums.at[pl.ds(1, 2 * X - 1)], sum_send, sum_recv).wait()
     total = jnp.sum(sums[...], axis=0)
-
-    @pl.loop(0, PAIRS)
-    def _(s):
-        heads[s, 1:2] = total
-        k = partner(s)
-
-        @pl.when(k != pair)
-        def _():
-            pltpu.make_async_remote_copy(
-                src_ref=heads.at[s], dst_ref=head_ref.at[pair],
-                send_sem=head_send, recv_sem=head_recv,
-                device_id={"dp": k * 2 + c}, device_id_type=MESH,
-            ).start()
-
-        @pl.when(k == pair)
-        def _():
-            pltpu.make_async_copy(heads.at[s], head_ref.at[pair], head_local).start()
-
-    @pl.loop(HELD, PAIRS)
-    def _(s):
-        give_back(s)
+    heads[...] += total[None]
+    for n in range(PAIRS):
+        send_back(heads, (head_send, head_recv), head_ref, head_local, n)
+
+    for n in range(HELD, PAIRS):
+        give_back(n)
 
     others = pl.ds(0, PAIRS - 1)
     whole(outgoing.at[others], grad_send, grad_recv.at[0, 0]).wait_send()
@@ -306,6 +306,12 @@
     pltpu.make_async_copy(heads.at[0], head_ref.at[pair], head_local).wait()
     whole(back_ref.at[others], back_send, back_recv).wait()
     whole(head_ref.at[others], head_send, head_recv).wait()
+
+    sums_ref[...] = jnp.sum(head_ref[...], axis=0)
+    for b in range(PAIRS):
+        k = owner_ref[0, b]
+        rows_ref[b] = back_ref[k]
+        scale_ref[b] = head_ref[k]
 
 
 def _fold(value):
@@ -322,15 +328,19 @@
         exchange_kernel,
         out_shape=(
             jax.ShapeDtypeStruct((PAIRS, ROWS, HALF), jnp.int32),
-            jax.ShapeDtypeStruct((PAIRS, 2, LANES), F32),
+            jax.ShapeDtypeStruct((PAIRS, 1, LANES), F32),
+            jax.ShapeDtypeStruct((1, LANES), F32),
         ),
         in_specs=[
             pl.BlockSpec(memory_space=pltpu.VMEM),
             pl.BlockSpec(memory_space=pltpu.HBM),
             pl.BlockSpec(memory_space=pltpu.HBM),
         ],
-        out_specs=[pl.BlockSpec(memory_space=pltpu.VMEM)] * 2,
+        out_specs=[pl.BlockSpec(memory_space=pltpu.VMEM)] * 3,
         scratch_shapes=[
+            pltpu.SMEM((1, PAIRS), jnp.int32),
+            pltpu.VMEM((PAIRS, ROWS, HALF), jnp.int32),
+            pltpu.VMEM((PAIRS, 1, LANES), F32),
             pltpu.VMEM(grads_words, BF16),
             pltpu.SMEM((PACKED,), jnp.int32),
             pltpu.VMEM((Z, Y, 2, ROWS, B), F32),
@@ -341,9 +351,10 @@
             pltpu.VMEM((2, Z, Y, ROWS, B), BF16),
             pltpu.VMEM((HALF, B), F32),
             pltpu.VMEM((PAIRS, ROWS, HALF), jnp.int32),
-            pltpu.VMEM((PAIRS, 2, LANES), F32),
+            pltpu.VMEM((PAIRS, 1, LANES), F32),
             pltpu.VMEM((2 * X, 1, LANES), F32),
             pltpu.VMEM((8, LANES), F32),
+            pltpu.SemaphoreType.DMA,
             pltpu.SemaphoreType.DMA,
             pltpu.SemaphoreType.DMA,
             pltpu.SemaphoreType.DMA,
@@ -371,25 +382,18 @@
 STEP = 4
 
 
-def update_kernel(owner_in, back_ref, head_ref, momentum_ref, new_hbm, direction_hbm, owner_ref, new, direction, scales, owner_sem, sem):
-    owner = pltpu.make_async_copy(owner_in, owner_ref, owner_sem)
-    owner.start()
+def update_kernel(rows_ref, scale_ref, sums_ref, momentum_ref, new_hbm, direction_hbm, new, direction, sem):
     lane = lax.broadcasted_iota(jnp.int32, (ROWS, LANES), 1)
-    diagonal = lane == lax.broadcasted_iota(jnp.int32, (ROWS, LANES), 0)
-    heads = head_ref[...]
-    totals = jnp.sum(heads, axis=0)[1:2]
-    grad = pltpu.roll(totals, 64, 1)
+    diagonal = lane == lax.broadcasted_iota(jnp.int32, (ROWS, LANES), 0) + 2 * PAIRS
+    totals = sums_ref[...]
+    grad = pltpu.roll(totals, LANES - PAIRS, 1)
     graft = jnp.sqrt(grad) / (jnp.sqrt(totals) + 1e-06) * (1.0 / (TOP * TOP))
-    for k in range(PAIRS):
-        top = jnp.broadcast_to(heads[k, 0:1], (ROWS, LANES))
-        top = jnp.sum(jnp.where(diagonal, top, 0.0), axis=1, keepdims=True)
-        scales[k] = jnp.broadcast_to(top, (ROWS, LANES))
-    owner.wait()
     copies = []
     for b in range(PAIRS):
-        k = owner_ref[0, b]
-        scale = scales[k] * jnp.broadcast_to(graft[:, b:b + 1], (ROWS, LANES))
-        words = back_ref[k]
+        top = jnp.where(diagonal, jnp.broadcast_to(scale_ref[b], (ROWS, LANES)), 0.0)
+        top = jnp.sum(top, axis=1, keepdims=True)
+        scale = jnp.broadcast_to(top, (ROWS, LANES)) * jnp.broadcast_to(graft[:, b:b + 1], (ROWS, LANES))
+        words = rows_ref[b]
         for h, code in enumerate(((words << 16) >> 16, words >> 16)):
             code = code.astype(F32)
             code = code * jnp.abs(code)
@@ -408,7 +412,7 @@
         copy.wait()
 
 
-def apply_update(owner, back, head, momentum):
+def apply_update(rows, scale, sums, momentum):
     return pl.pallas_call(
         update_kernel,
         out_shape=(
@@ -416,29 +420,26 @@
             jax.ShapeDtypeStruct((PAIRS, ROWS, B), BF16),
         ),
         in_specs=[
-            pl.BlockSpec(memory_space=pl.ANY),
+            pl.BlockSpec(memory_space=pltpu.VMEM),
             pl.BlockSpec(memory_space=pltpu.VMEM),
             pl.BlockSpec(memory_space=pltpu.VMEM),
             pl.BlockSpec(memory_space=pltpu.VMEM),
         ],
         out_specs=[pl.BlockSpec(memory_space=pltpu.HBM)] * 2,
         scratch_shapes=[
-            pltpu.SMEM((1, PAIRS), jnp.int32),
             pltpu.VMEM((PAIRS, ROWS, B), F32),
             pltpu.VMEM((PAIRS, ROWS, B), BF16),
-            pltpu.VMEM((PAIRS, ROWS, LANES), F32),
-            pltpu.SemaphoreType.DMA,
             pltpu.SemaphoreType.DMA((2, PAIRS // STEP)),
         ],
         compiler_params=pltpu.CompilerParams(vmem_limit_bytes=24 * 1024 * 1024),
         name="update",
-    )(owner, back, head, momentum)
+    )(rows, scale, sums, momentum)
 
 
 def per_device(grads, momentum, root_factors, owner_table):
     factor = root_factors.reshape(Z, Y, 2, ROWS, B)
-    back, head = exchange(owner_table, grads[0], factor)
-    new_momentum, direction = apply_update(owner_table, back, head, momentum[0])
+    rows, scale, sums = exchange(owner_table, grads[0], factor)
+    new_momentum, direction = apply_update(rows, scale, sums, momentum[0])
     return (new_momentum[None], direction[None])
 
 

time: 64.7 us -> 64.6 us (level)
  Pallas kernels: 62.9 us -> 62.2 us
where the time goes in v5:
time: 64.6 us; the launch traced here: 63.5 us
  Pallas kernels  62.2 us (96%)
  between operations  0.66 us (1%)
  local copies, waits for them, and re-layouts  0.65 us (1%)
    pallas_call x1, Pallas kernels, exchange(): pl.pallas_call(exchange_kernel, out_shape=(jax.ShapeDtypeStruct((PAIRS, R...  60.2 us
    pallas_call x1, Pallas kernels, apply_update(): pl.pallas_call(update_kernel, out_shape=(jax.ShapeDtypeStruct((PAIRS, ROW...  2.02 us

profile of v5, /device:TPU:1, one launch (start us, length us, event | category | flops | bytes accessed | tf_op | source)
XLA Modules:
  0.0 63.5 jit_solution(11641310559072958015)
XLA Ops:
  0.6 0.0 copy-start.1
  0.6 0.6 %copy-done.1 = s32[1,32]{1,0:T(1,128)S(1)} copy-done((s32[1,32]{1,0:T(1,128)S(1)}, s32[1,32]{1,0:T(1,128)}, u32[]{:S(2)}) %copy-start.1) | copy-done | bytes 152
  1.3 0.0 copy-start
  1.3 60.2 %exchange.1 = (s32[32,16,512]{2,1,0:T(8,128)S(1)}, f32[32,1,128]{2,1,0:T(1,128)S(1)}, f32[1,128]{1,0:T(1,128)S(1)}) custom-call(s32[1,32]{1,0:T(1,128)S(1)} %copy-done.1, bf16[32,16,1024]{2,1,0:T(8,128)(2,1)} %bitcast.7, f32[8,4,2,16,1024]{4,3,2,1,0:T(8,128)} %bitcast.6), custom_call_target="tpu_custom_call" | custom-call | tf_op jit(solution)/shard_map/exchange/pallas_call | solution.py:327
  61.5 0.0 copy-done
  61.5 2.0 %update.1 = (f32[32,16,1024]{2,1,0:T(8,128)}, bf16[32,16,1024]{2,1,0:T(8,128)(2,1)}) custom-call(s32[32,16,512]{2,1,0:T(8,128)S(1)} %get-tuple-element.7.rows_ref, f32[32,1,128]{2,1,0:T(1,128)S(1)} %get-tuple-element.8.scale_ref, f32[1,128]{1,0:T(1,128)S(1)} %get-tuple-element.9.sums_ref, f32[32,16,1024]{2,1,0:T(8,128)S(1)} %bitcast.5), custom_call_target="tpu_custom_call" | custom-call | tf_op jit(solution)/shard_map/update/pallas_call | solution.py:416
Async XLA Ops:
  0.6 0.7 %copy-start.1 = (s32[1,32]{1,0:T(1,128)S(1)}, s32[1,32]{1,0:T(1,128)}, u32[]{:S(2)}) copy-start(s32[1,32]{1,0:T(1,128)} %owner_rows.1) | copy-start | bytes 388
  1.3 60.2 %copy-start = (f32[1,32,16,1024]{3,2,1,0:T(8,128)S(1)}, f32[1,32,16,1024]{3,2,1,0:T(8,128)}, u32[]{:S(2)}) copy-start(f32[1,32,16,1024]{3,2,1,0:T(8,128)} %param.5) | copy-start | bytes 6291460
